TPU v7x, 512 devices: a whole 4x8x8 slice. The times are simulated.
512 devices in a mesh: expert: 128 (over z, y, core), replica: 4 (over x).
Axes of the slice: x: 4, y: 8, z: 8, core: 2. Of those that a mesh axis runs over, the one named last changes fastest.
Arguments:
- tokens: bfloat16 [16384, 6144], P('expert', 'replica'), may hold values from -6 to 6
- probe: bfloat16 [16384, 6144], P('expert', 'replica'), may hold values from -6 to 6
- cotangent: bfloat16 [16384, 1024], P('expert'), may hold values from -6 to 6
- expert_ids: int32 [16384, 1], P('expert'), may hold values from 0 to 127; in each aligned block of 128 rows (0 to 127, 128 to 255, ...) at most 2 rows name the same one
- weight: bfloat16 [128, 6144, 1024], P('expert', 'replica'), may hold values from -0.078125 to 0.078125
Outputs:
- grad_rows: bfloat16 [16384, 6144], P('expert', 'replica')
- hv_rows: bfloat16 [16384, 6144], P('expert', 'replica')
Inputs may be any that keep to these rules, and one draw needn't show every extreme that they name: `expert_ids`: among the 128 tokens of one index of the expert axis at most 2 name the same expert; in every draw some index has exactly 2 tokens that name one expert.
All inputs are finite; a program needn't handle non-finite values.
Results may differ from a plain program's by a relative error of at most 0.0049.
Values may be sent and summed in bfloat16 or wider, within the bound.
A program may use at most 64 MiB of HBM per device.

v0:
```python
import jax
import jax.numpy as jnp
from jax import lax
from jax.sharding import PartitionSpec as P


def derivatives(pre):
    sig = jax.nn.sigmoid(pre)
    first = sig * (1.0 + pre * (1.0 - sig))
    second = sig * (1.0 - sig) * (2.0 + pre * (1.0 - 2.0 * sig))
    return (first, second)


def shards(tokens, probe, cotangent, expert_ids, weight):
    ids = expert_ids[:, 0]
    count = ids.shape[0]
    experts = lax.axis_size("expert")
    capacity = 2 * max(1, count // experts)
    width = tokens.shape[1]
    owner = (ids[:, None] == jnp.arange(experts, dtype=jnp.int32)[None, :]).astype(jnp.float32)
    positions = jnp.arange(count, dtype=jnp.int32)
    earlier = (positions[:, None] > positions[None, :]).astype(jnp.float32)
    before = jnp.dot(
        earlier, owner, precision=lax.Precision.HIGHEST, preferred_element_type=jnp.float32
    )
    place = jnp.sum(owner * before, axis=1).astype(jnp.int32)
    slot = ids * capacity + place
    route = (jnp.arange(experts * capacity, dtype=jnp.int32)[:, None] == slot[None, :]).astype(
        jnp.bfloat16
    )
    send_x = (
        jnp.dot(route, tokens, preferred_element_type=jnp.float32)
        .astype(jnp.bfloat16)
        .reshape(experts, capacity, width)
    )
    send_p = (
        jnp.dot(route, probe, preferred_element_type=jnp.float32)
        .astype(jnp.bfloat16)
        .reshape(experts, capacity, width)
    )
    send_c = (
        jnp.dot(route, cotangent, preferred_element_type=jnp.float32)
        .astype(jnp.bfloat16)
        .reshape(experts, capacity, cotangent.shape[1])
    )
    matrix = weight[0]
    dims = (((1,), (1,)), ((), ()))
    recv_x = lax.all_to_all(send_x, "expert", split_axis=0, concat_axis=0, tiled=True)
    recv_p = lax.all_to_all(send_p, "expert", split_axis=0, concat_axis=0, tiled=True)
    recv_c = lax.all_to_all(send_c, "expert", split_axis=0, concat_axis=0, tiled=True)
    sources = recv_x.shape[0]
    items = recv_x.shape[1]
    rows_x = recv_x.reshape(sources * items, width)
    rows_p = recv_p.reshape(sources * items, width)
    rows_c = recv_c.reshape(sources * items, recv_c.shape[2]).astype(jnp.float32)
    pre_part = jnp.dot(rows_x, matrix, preferred_element_type=jnp.float32)
    dot_part = jnp.dot(rows_p, matrix, preferred_element_type=jnp.float32)
    pre, pre_dot = lax.psum((pre_part, dot_part), "replica")
    first_d, second_d = derivatives(pre)
    first = (rows_c * first_d).astype(jnp.bfloat16)
    second = (rows_c * second_d * pre_dot).astype(jnp.bfloat16)
    grads = lax.dot_general(first, matrix, dims, preferred_element_type=jnp.float32)
    hvs = lax.dot_general(second, matrix, dims, preferred_element_type=jnp.float32)
    grad_back = grads.astype(jnp.bfloat16).reshape(sources, items, width)
    hv_back = hvs.astype(jnp.bfloat16).reshape(sources, items, width)
    back_grad = lax.all_to_all(grad_back, "expert", split_axis=0, concat_axis=0, tiled=True)
    back_hv = lax.all_to_all(hv_back, "expert", split_axis=0, concat_axis=0, tiled=True)
    combine = (((0,), (0,)), ((), ()))
    grad_rows = lax.dot_general(
        route,
        back_grad.reshape(experts * capacity, width),
        combine,
        preferred_element_type=jnp.float32,
    ).astype(jnp.bfloat16)
    hv_rows = lax.dot_general(
        route,
        back_hv.reshape(experts * capacity, width),
        combine,
        preferred_element_type=jnp.float32,
    ).astype(jnp.bfloat16)
    return (grad_rows, hv_rows)


def solution(mesh):
    in_specs = (
        P("expert", "replica"),
        P("expert", "replica"),
        P("expert", None),
        P("expert", None),
        P("expert", "replica", None),
    )
    out_specs = (P("expert", "replica"), P("expert", "replica"))
    return jax.shard_map(shards, mesh=mesh, in_specs=in_specs, out_specs=out_specs, check_vma=False)
```

profile of v0, /device:TPU:1, one launch (start us, length us, event | category | flops | bytes accessed | tf_op | source)
XLA Modules:
  0.0 250.0 jit_solution(8975505903949570679)
XLA Ops:
  7.2 0.0 copy-start
  7.2 0.0 copy-start.1
  7.2 1.0 fusion.14
  8.2 0.7 convert_add_fusion
  8.9 2.2 convolution_convert_fusion
  11.1 2.8 %reshape.48 = bf16[128,2,1536]{2,1,0:T(2,128)(2,1)} reshape(bf16[256,1536]{1,0:T(8,128)(2,1)} %convolution_convert_fusion) | data formatting | bytes 1572864 | tf_op jit(solution)/shard_map/reshape | solution.py:39
  14.0 18.8 %all-to-all-start.3 = ((bf16[128,2,1536]{2,1,0:T(2,128)(2,1)}), bf16[128,2,1536]{2,1,0:T(2,128)(2,1)}, u32[]{:S(2)}, u32[]{:S(2)}) async-start(bf16[128,2,1536]{2,1,0:T(2,128)(2,1)} %reshape.48), calls=%async_computation.3 | async-start | bytes 1572864 | tf_op jit(solution)/shard_map/all_to_all | solution.py:49
  32.8 0.0 copy-done.1
  32.8 1.3 convolution_convert_fusion.1
  34.1 2.8 %reshape.44 = bf16[128,2,1536]{2,1,0:T(2,128)(2,1)} reshape(bf16[256,1536]{1,0:T(8,128)(2,1)} %convolution_convert_fusion.1) | data formatting | bytes 1572864 | tf_op jit(solution)/shard_map/reshape | solution.py:34
  36.9 21.5 %all-to-all-done.3 = bf16[128,2,1536]{2,1,0:T(2,128)(2,1)} async-done(((bf16[128,2,1536]{2,1,0:T(2,128)(2,1)}), bf16[128,2,1536]{2,1,0:T(2,128)(2,1)}, u32[]{:S(2)}, u32[]{:S(2)}) %all-to-all-start.3) | async-done | bytes 786464 | tf_op jit(solution)/shard_map/all_to_all | solution.py:49
  58.5 6.4 %all-to-all-start.1 = ((bf16[128,2,1536]{2,1,0:T(2,128)(2,1)}), bf16[128,2,1536]{2,1,0:T(2,128)(2,1)}, u32[]{:S(2)}, u32[]{:S(2)}) async-start(bf16[128,2,1536]{2,1,0:T(2,128)(2,1)} %reshape.44), calls=%async_computation.1 | async-start | bytes 1572864 | tf_op jit(solution)/shard_map/all_to_all | solution.py:48
  64.8 0.0 all-reduce.3.cloned.1.call-start
  64.9 3.0 %reshape.49 = bf16[256,1536]{1,0:T(8,128)(2,1)} reshape(bf16[128,2,1536]{2,1,0:T(2,128)(2,1)} %all-to-all-done.3) | data formatting | bytes 1572864 | tf_op jit(solution)/shard_map/reshape | solution.py:54
  67.9 0.0 copy-done
  67.9 3.1 %fusion.2 = f32[256,1024]{1,0:T(8,128)} fusion(bf16[256,1536]{1,0:T(8,128)(2,1)} %reshape.49, bf16[1,1536,1024]{2,1,0:T(8,128)(2,1)S(1)} %copy-done), kind=kOutput, calls=%fused_computation.2 | convolution fusion | flops 805306368 | bytes 4980736 | tf_op jit(solution)/shard_map/dot_general | solution.py:57
  71.0 19.2 %all-to-all-done.1 = bf16[128,2,1536]{2,1,0:T(2,128)(2,1)} async-done(((bf16[128,2,1536]{2,1,0:T(2,128)(2,1)}), bf16[128,2,1536]{2,1,0:T(2,128)(2,1)}, u32[]{:S(2)}, u32[]{:S(2)}) %all-to-all-start.1) | async-done | bytes 786464 | tf_op jit(solution)/shard_map/all_to_all | solution.py:48
  90.2 2.9 %reshape.45 = bf16[256,1536]{1,0:T(8,128)(2,1)} reshape(bf16[128,2,1536]{2,1,0:T(2,128)(2,1)} %all-to-all-done.1) | data formatting | bytes 1572864 | tf_op jit(solution)/shard_map/reshape | solution.py:53
  93.2 0.0 copy-start.2
  93.2 3.1 %fusion.6 = f32[256,1024]{1,0:T(8,128)} fusion(bf16[256,1536]{1,0:T(8,128)(2,1)} %reshape.45, bf16[1,1536,1024]{2,1,0:T(8,128)(2,1)S(1)} %copy-done), kind=kOutput, calls=%fused_computation.6 | convolution fusion | flops 805306368 | bytes 4980736 | tf_op jit(solution)/shard_map/dot_general | solution.py:56
  96.3 0.0 all-reduce.3.cloned.1.call-update
  96.3 0.0 copy-done.2
  96.4 1.1 convolution_convert_fusion.4
  97.4 2.0 reshape.43
  99.5 26.8 %all_to_all.25 = bf16[128,2,1024]{2,1,0:T(2,128)(2,1)} all-to-all(bf16[128,2,1024]{2,1,0:T(2,128)(2,1)} %reshape.43), channel_id=1, replica_groups=mesh['expert'=128,'replica'=4] {'expert'}, dimensions={0} | all-to-all | bytes 1048576 | tf_op jit(solution)/shard_map/all_to_all | solution.py:50
  126.3 2.1 reshape.52
  128.4 30.4 %all-reduce.3.cloned.1.call-done = (f32[256,1024]{1,0:T(8,128)}, f32[256,1024]{1,0:T(8,128)}) async-done(((f32[256,1024]{1,0:T(8,128)}, f32[256,1024]{1,0:T(8,128)}), (f32[256,1024]{1,0:T(8,128)}, f32[256,1024]{1,0:T(8,128)})) %all-reduce.3.cloned.1.call-update) | async-done | bytes 2097168 | tf_op jit(solution)/shard_map/psum | solution.py:58
  158.8 4.2 %fusion.11 = bf16[256,1536]{1,0:T(8,128)(2,1)} fusion(bf16[1,1536,1024]{2,1,0:T(8,128)(2,1)S(1)} %copy-done, f32[256,1024]{1,0:T(8,128)} %get-tuple-element.3, f32[256,1024]{1,0:T(8,128)} %reshape.52, f32[256,1024]{1,0:T(8,128)} %get-tuple-element.2), kind=kOutput, calls=%fused_computation.9 | convolution fusion | flops 809107456 | bytes 7077888 | tf_op jit(solution)/shard_map/dot_general | solution.py:63
  163.1 2.8 %reshape.50 = bf16[128,2,1536]{2,1,0:T(2,128)(2,1)} reshape(bf16[256,1536]{1,0:T(8,128)(2,1)} %fusion.11) | data formatting | bytes 1572864 | tf_op jit(solution)/shard_map/reshape | solution.py:65
  165.9 14.7 %all-to-all-start.4 = ((bf16[128,2,1536]{2,1,0:T(2,128)(2,1)}), bf16[128,2,1536]{2,1,0:T(2,128)(2,1)}, u32[]{:S(2)}, u32[]{:S(2)}) async-start(bf16[128,2,1536]{2,1,0:T(2,128)(2,1)} %reshape.50), calls=%async_computation.4 | async-start | bytes 1572864 | tf_op jit(solution)/shard_map/all_to_all | solution.py:67
  180.6 3.6 %fusion.8 = bf16[256,1536]{1,0:T(8,128)(2,1)} fusion(bf16[1,1536,1024]{2,1,0:T(8,128)(2,1)S(1)} %copy-done, f32[256,1024]{1,0:T(8,128)} %reshape.52, f32[256,1024]{1,0:T(8,128)} %get-tuple-element.2), kind=kOutput, calls=%fused_computation.8 | convolution fusion | flops 808058880 | bytes 6029312 | tf_op jit(solution)/shard_map/dot_general | solution.py:62
  184.2 2.8 %reshape.46 = bf16[128,2,1536]{2,1,0:T(2,128)(2,1)} reshape(bf16[256,1536]{1,0:T(8,128)(2,1)} %fusion.8) | data formatting | bytes 1572864 | tf_op jit(solution)/shard_map/reshape | solution.py:64
  187.0 19.2 %all-to-all-done.4 = bf16[128,2,1536]{2,1,0:T(2,128)(2,1)} async-done(((bf16[128,2,1536]{2,1,0:T(2,128)(2,1)}), bf16[128,2,1536]{2,1,0:T(2,128)(2,1)}, u32[]{:S(2)}, u32[]{:S(2)}) %all-to-all-start.4) | async-done | bytes 786464 | tf_op jit(solution)/shard_map/all_to_all | solution.py:67
  206.2 6.6 %all-to-all-start.2 = ((bf16[128,2,1536]{2,1,0:T(2,128)(2,1)}), bf16[128,2,1536]{2,1,0:T(2,128)(2,1)}, u32[]{:S(2)}, u32[]{:S(2)}) async-start(bf16[128,2,1536]{2,1,0:T(2,128)(2,1)} %reshape.46), calls=%async_computation.2 | async-start | bytes 1572864 | tf_op jit(solution)/shard_map/all_to_all | solution.py:66
  212.8 3.0 %reshape.51 = bf16[256,1536]{1,0:T(8,128)(2,1)} reshape(bf16[128,2,1536]{2,1,0:T(2,128)(2,1)} %all-to-all-done.4) | data formatting | bytes 1572864 | tf_op jit(solution)/shard_map/reshape | solution.py:77
  215.8 2.2 convolution_convert_fusion.2
  218.0 20.0 %all-to-all-done.2 = bf16[128,2,1536]{2,1,0:T(2,128)(2,1)} async-done(((bf16[128,2,1536]{2,1,0:T(2,128)(2,1)}), bf16[128,2,1536]{2,1,0:T(2,128)(2,1)}, u32[]{:S(2)}, u32[]{:S(2)}) %all-to-all-start.2) | async-done | bytes 786464 | tf_op jit(solution)/shard_map/all_to_all | solution.py:66
  238.0 2.9 %reshape.47 = bf16[256,1536]{1,0:T(8,128)(2,1)} reshape(bf16[128,2,1536]{2,1,0:T(2,128)(2,1)} %all-to-all-done.2) | data formatting | bytes 1572864 | tf_op jit(solution)/shard_map/reshape | solution.py:71
  240.9 2.2 convolution_convert_fusion.3
Async XLA Ops:
  7.2 60.7 %copy-start = (bf16[1,1536,1024]{2,1,0:T(8,128)(2,1)S(1)}, bf16[1,1536,1024]{2,1,0:T(8,128)(2,1)}, u32[]{:S(2)}) copy-start(bf16[1,1536,1024]{2,1,0:T(8,128)(2,1)} %param.9) | copy-start | bytes 9437188
  7.2 25.6 %copy-start.1 = (bf16[128,1536]{1,0:T(8,128)(2,1)S(1)}, bf16[128,1536]{1,0:T(8,128)(2,1)}, u32[]{:S(2)}) copy-start(bf16[128,1536]{1,0:T(8,128)(2,1)} %param.5) | copy-start | bytes 1179652
  14.0 44.5 %all-to-all-start.3 = ((bf16[128,2,1536]{2,1,0:T(2,128)(2,1)}), bf16[128,2,1536]{2,1,0:T(2,128)(2,1)}, u32[]{:S(2)}, u32[]{:S(2)}) async-start(bf16[128,2,1536]{2,1,0:T(2,128)(2,1)} %reshape.48), calls=%async_computation.3 | async-start | bytes 1572864 | tf_op jit(solution)/shard_map/all_to_all | solution.py:49
  58.5 31.8 %all-to-all-start.1 = ((bf16[128,2,1536]{2,1,0:T(2,128)(2,1)}), bf16[128,2,1536]{2,1,0:T(2,128)(2,1)}, u32[]{:S(2)}, u32[]{:S(2)}) async-start(bf16[128,2,1536]{2,1,0:T(2,128)(2,1)} %reshape.44), calls=%async_computation.1 | async-start | bytes 1572864 | tf_op jit(solution)/shard_map/all_to_all | solution.py:48
  64.8 94.0 %all-reduce.3.cloned.1.call-start = ((), (), s32[]{:S(2)}) async-start(), calls=%async_computation.5 | async-start | bytes 4194304 | tf_op jit(solution)/shard_map/psum | solution.py:58
  93.2 3.2 %copy-start.2 = (bf16[128,1024]{1,0:T(8,128)(2,1)S(1)}, bf16[128,1024]{1,0:T(8,128)(2,1)}, u32[]{:S(2)}) copy-start(bf16[128,1024]{1,0:T(8,128)(2,1)} %param.7) | copy-start | bytes 786436
  165.9 40.3 %all-to-all-start.4 = ((bf16[128,2,1536]{2,1,0:T(2,128)(2,1)}), bf16[128,2,1536]{2,1,0:T(2,128)(2,1)}, u32[]{:S(2)}, u32[]{:S(2)}) async-start(bf16[128,2,1536]{2,1,0:T(2,128)(2,1)} %reshape.50), calls=%async_computation.4 | async-start | bytes 1572864 | tf_op jit(solution)/shard_map/all_to_all | solution.py:67
  206.2 31.8 %all-to-all-start.2 = ((bf16[128,2,1536]{2,1,0:T(2,128)(2,1)}), bf16[128,2,1536]{2,1,0:T(2,128)(2,1)}, u32[]{:S(2)}, u32[]{:S(2)}) async-start(bf16[128,2,1536]{2,1,0:T(2,128)(2,1)} %reshape.46), calls=%async_computation.2 | async-start | bytes 1572864 | tf_op jit(solution)/shard_map/all_to_all | solution.py:66
Sparse Core Ops, SparseCore 0:
  96.5 62.2 all-reduce.2
where the time goes:
time: 251 us; the launch traced here: 250 us
  waiting for transfers between devices  110 us (44%)
  starting transfers between devices  46.5 us (19%)
  local copies, waits for them, and re-layouts  27.4 us (11%)
  blocking collectives  26.8 us (11%)
  matrix products  24.1 us (10%)
  between operations  14.1 us (6%)
    psum x1, waiting for transfers between devices, shards(): pre, pre_dot = lax.psum((pre_part, dot_part), 'replica')  30.4 us
    all_to_all x1, blocking collectives, shards(): lax.all_to_all(send_c, 'expert', split_axis=0, concat_axis=0, tiled=True)  26.8 us
    all_to_all x1, waiting for transfers between devices, shards(): lax.all_to_all(send_p, 'expert', split_axis=0, concat_axis=0, tiled=True)  21.5 us
    all_to_all x1, waiting for transfers between devices, shards(): lax.all_to_all(grad_back, 'expert', split_axis=0, concat_axis=0, tiled=True)  20 us
    all_to_all x1, waiting for transfers between devices, shards(): lax.all_to_all(send_x, 'expert', split_axis=0, concat_axis=0, tiled=True)  19.2 us
    all_to_all x1, waiting for transfers between devices, shards(): lax.all_to_all(hv_back, 'expert', split_axis=0, concat_axis=0, tiled=True)  19.2 us
    all_to_all x1, starting transfers between devices, shards(): lax.all_to_all(send_p, 'expert', split_axis=0, concat_axis=0, tiled=True)  18.8 us
    all_to_all x1, starting transfers between devices, shards(): lax.all_to_all(hv_back, 'expert', split_axis=0, concat_axis=0, tiled=True)  14.7 us
  transfers between devices with their start and end apart: 5, of which 5 were waited for; matrix products, arithmetic and copies ran while one was open for 11% of the time, Pallas kernels for 0%

commit v1 on v0

v1 whole, which is shorter than its diff:
```python
import functools

import jax
import jax.numpy as jnp
from jax import lax
from jax.experimental import pallas as pl
from jax.experimental.pallas import tpu as pltpu
from jax.sharding import PartitionSpec as P

MESH = pl.DeviceIdType.MESH
F32 = jnp.float32
BF16 = jnp.bfloat16


def mm(a, b):
    return jnp.dot(a, b, preferred_element_type=F32)


def iota(shape, dim):
    return lax.broadcasted_iota(jnp.int32, shape, dim)


def transpose_matrix(a, b):
    row, col = iota((a * b, a * b), 0), iota((a * b, a * b), 1)
    return jnp.where((row % b) * a + row // b == col, 1.0, 0.0).astype(BF16)


def kernel(
    zs, ys, reps,
    x_ref, p_ref, cot_ref, ids_ref, w_hbm,
    grad_ref, hv_ref,
    w, fsend, frecv, csend, crecv, part, rsrecv, act, bsend, brecv, rows,
    to_blocks, from_blocks, cot_to, cot_from,
    w_sem, f_ss, f_rs, c_ss, c_rs, r_ss, r_rs, a_ss, a_rs, b_ss, b_rs,
):
    experts = 2 * zs * ys
    m = 2 * zs
    n, width = x_ref.shape
    kc = width // 4
    ffq = part.shape[2] // reps
    me = lax.axis_index("expert")
    rep = lax.axis_index("replica")
    core = lax.rem(me, 2)
    y = lax.rem(me // 2, ys)
    z = me // (2 * ys)

    def dest(c, i):
        dz, rc = i // 2, lax.rem(i, 2)
        zz, yy = lax.rem(z + dz, zs), lax.rem(y + dz + c, ys)
        return (zz * ys + yy) * 2 + lax.rem(core + rc, 2)

    def source(c, i):
        dz, rc = i // 2, lax.rem(i, 2)
        zz, yy = lax.rem(z + zs - dz, zs), lax.rem(y + (zs + 2) * ys - dz - c, ys)
        return (zz * ys + yy) * 2 + lax.rem(core + rc, 2)

    w_copy = pltpu.make_async_copy(w_hbm, w, w_sem)
    w_copy.start()

    barrier = pltpu.get_barrier_semaphore()

    def greet(i, carry):
        pl.semaphore_signal(
            barrier, inc=1, device_id=(lax.rem(me + i, experts), rep), device_id_type=MESH
        )
        return carry

    for j in range(1, reps):
        pl.semaphore_signal(
            barrier, inc=1, device_id=(me, lax.rem(rep + j, reps)), device_id_type=MESH
        )
    lax.fori_loop(1, experts, greet, 0)

    ids_col = ids_ref[...]
    row, col = iota((n, n), 0), iota((n, n), 1)
    ids_row = jnp.sum(
        jnp.where(row == col, ids_col.astype(F32), 0.0), axis=0, keepdims=True
    ).astype(jnp.int32)
    same = ids_col == ids_row
    slot_row = jnp.sum(
        jnp.where(same & (row < col), 1.0, 0.0), axis=0, keepdims=True
    ).astype(jnp.int32)
    slot_col = jnp.sum(
        jnp.where(same & (col < row), 1.0, 0.0), axis=1, keepdims=True
    ).astype(jnp.int32)

    def target(ids, slot):
        to_core, to_y, to_z = ids % 2, (ids // 2) % ys, ids // (2 * ys)
        dz = (to_z - z + zs) % zs
        c = (to_y - y - dz + (zs + 2) * ys) % ys
        return c * (2 * m) + slot * m + dz * 2 + (to_core + core) % 2

    tgt_row = target(ids_row, slot_row)
    tgt_col = target(ids_col, slot_col)

    to_blocks[...] = transpose_matrix(m, 16)
    from_blocks[...] = transpose_matrix(16, m)
    cot_to[...] = transpose_matrix(m, 4)
    cot_from[...] = transpose_matrix(4, m)

    def whole(ref, c, sem, own):
        if not own:
            pltpu.make_async_copy(ref.at[c], ref.at[c], sem.at[c]).wait()
            return

        @pl.when(c == 0)
        def _():
            some = ref.at[0, pl.ds(1, m - 1)]
            pltpu.make_async_copy(some, some, sem.at[0]).wait()

        @pl.when(c > 0)
        def _():
            pltpu.make_async_copy(ref.at[c], ref.at[c], sem.at[c]).wait()

    def blocks(stacked):
        tall = jnp.concatenate([stacked[:, k * kc:(k + 1) * kc] for k in range(4)], axis=0)
        return mm(to_blocks[...], tall).astype(BF16).reshape(m, 16, kc)

    def unblock(block):
        tall = mm(from_blocks[...], block.reshape(m * 16, kc)).astype(BF16)
        return jnp.concatenate([tall[k * 4 * m:(k + 1) * 4 * m] for k in range(4)], axis=1)

    def pack(c):
        route = jnp.where(iota((2 * m, n), 0) + c * (2 * m) == tgt_row, 1.0, 0.0).astype(BF16)
        xs = mm(route, x_ref[...]).astype(BF16)
        ps = mm(route, p_ref[...]).astype(BF16)
        block = blocks(jnp.concatenate([xs, ps], axis=0))
        fsend[c] = block
        mine = cot_ref[:, pl.ds(pl.multiple_of(rep * ffq, ffq), ffq)]
        cs = mm(route, mine).astype(BF16)
        half = ffq // 2
        tall = jnp.concatenate([cs[:, :half], cs[:, half:]], axis=0)
        cblock = mm(cot_to[...], tall).astype(BF16).reshape(m, 4, half)
        csend[c] = cblock

        @pl.when(c == 0)
        def _():
            frecv[0, 0] = block[0]
            crecv[0, 0] = cblock[0]

    def send(c, first):
        def one(i, carry):
            to = (dest(c, i), rep)
            pltpu.make_async_remote_copy(
                src_ref=fsend.at[c, i], dst_ref=frecv.at[c, i],
                send_sem=f_ss.at[c], recv_sem=f_rs.at[c],
                device_id=to, device_id_type=MESH,
            ).start()
            pltpu.make_async_remote_copy(
                src_ref=csend.at[c, i], dst_ref=crecv.at[c, i],
                send_sem=c_ss.at[c], recv_sem=c_rs.at[c],
                device_id=to, device_id_type=MESH,
            ).start()
            return carry

        lax.fori_loop(first, m, one, 0)

    pack(0)
    pl.semaphore_wait(barrier, experts - 1 + reps - 1)
    send(0, 1)

    def dispatch(c, carry):
        pack(c)
        send(c, 0)
        return carry

    lax.fori_loop(1, ys, dispatch, 0)
    w_copy.wait()

    def quarter(r):
        return pl.ds(pl.multiple_of(r * ffq, ffq), ffq)

    def project(c):
        whole(frecv, c, f_rs, True)
        part[c] = mm(unblock(frecv[c]), w[...])
        for j in range(1, reps):
            to = lax.rem(rep + j, reps)
            pltpu.make_async_remote_copy(
                src_ref=part.at[c, :, quarter(to)], dst_ref=rsrecv.at[c, j - 1],
                send_sem=r_ss.at[c], recv_sem=r_rs.at[c],
                device_id=(me, to), device_id_type=MESH,
            ).start()

    def activate(c):
        whole(rsrecv, c, r_rs, False)
        whole(crecv, c, c_rs, True)
        total = part[c, :, quarter(rep)]
        for j in range(reps - 1):
            total = total + rsrecv[c, j]
        pre, pre_dot = total[:2 * m], total[2 * m:]
        half = ffq // 2
        tall = mm(cot_from[...], crecv[c].reshape(4 * m, half))
        cot = jnp.concatenate([tall[:2 * m], tall[2 * m:]], axis=1)
        sig = 1.0 / (1.0 + jnp.exp(-pre))
        first = cot * (sig * (1.0 + pre * (1.0 - sig)))
        second = cot * (sig * (1.0 - sig) * (2.0 + pre * (1.0 - 2.0 * sig))) * pre_dot
        act[c, :, quarter(rep)] = jnp.concatenate([first, second], axis=0).astype(BF16)
        for j in range(1, reps):
            to = lax.rem(rep + j, reps)
            pltpu.make_async_remote_copy(
                src_ref=act.at[c, :, quarter(rep)], dst_ref=act.at[c, :, quarter(rep)],
                send_sem=a_ss.at[c], recv_sem=a_rs.at[c],
                device_id=(me, to), device_id_type=MESH,
            ).start()

    def others(ref, c, sem):
        some = ref.at[c, :, pl.ds(0, (reps - 1) * ffq)]
        pltpu.make_async_copy(some, some, sem.at[c]).wait()

    def give_back(c):
        others(act, c, a_rs)
        back = lax.dot_general(
            act[c], w[...], (((1,), (1,)), ((), ())), preferred_element_type=F32
        ).astype(BF16)
        block = blocks(back)
        bsend[c] = block

        @pl.when(c == 0)
        def _():
            brecv[0, 0] = block[0]

        def one(i, carry):
            @pl.when(c + i > 0)
            def _():
                pltpu.make_async_remote_copy(
                    src_ref=bsend.at[c, i], dst_ref=brecv.at[c, i],
                    send_sem=b_ss.at[c], recv_sem=b_rs.at[c],
                    device_id=(source(c, i), rep), device_id_type=MESH,
                ).start()
            return carry

        lax.fori_loop(0, m, one, 0)

    def step(s, carry):
        @pl.when(s < ys)
        def _():
            project(s)

        @pl.when((s >= 1) & (s < ys + 1))
        def _():
            activate(s - 1)

        @pl.when(s >= 2)
        def _():
            give_back(s - 2)

        return carry

    lax.fori_loop(0, ys + 2, step, 0)

    def collect(c, carry):
        whole(brecv, c, b_rs, True)
        got = unblock(brecv[c])
        at = pl.ds(pl.multiple_of(c * 2 * m, 2 * m), 2 * m)
        rows[0, at, :] = got[:2 * m]
        rows[1, at, :] = got[2 * m:]
        return carry

    lax.fori_loop(0, ys, collect, 0)

    pick = jnp.where(iota((n, 2 * m * ys), 1) == tgt_col, 1.0, 0.0).astype(BF16)
    grad_ref[...] = mm(pick, rows[0]).astype(BF16)
    hv_ref[...] = mm(pick, rows[1]).astype(BF16)

    def drain(c, carry):
        whole(fsend, c, f_ss, True)
        whole(csend, c, c_ss, True)
        whole(bsend, c, b_ss, True)
        others(part, c, r_ss)
        others(act, c, a_ss)
        return carry

    lax.fori_loop(0, ys, drain, 0)


def solution(mesh):
    experts, reps = mesh.shape["expert"], mesh.shape["replica"]
    zs = {128: 8, 8: 2}[experts]
    ys = experts // (2 * zs)
    m = 2 * zs

    def shards(tokens, probe, cotangent, expert_ids, weight):
        n, width = tokens.shape
        ff = weight.shape[2]
        ffq = ff // reps
        kc = width // 4
        vmem = pl.BlockSpec(memory_space=pltpu.VMEM)
        dma = pltpu.SemaphoreType.DMA
        return pl.pallas_call(
            functools.partial(kernel, zs, ys, reps),
            out_shape=[jax.ShapeDtypeStruct((n, width), BF16)] * 2,
            in_specs=[vmem] * 4 + [pl.BlockSpec(memory_space=pl.ANY)],
            out_specs=[vmem] * 2,
            scratch_shapes=[
                pltpu.VMEM((width, ff), BF16),
                pltpu.VMEM((ys, m, 16, kc), BF16),
                pltpu.VMEM((ys, m, 16, kc), BF16),
                pltpu.VMEM((ys, m, 4, ffq // 2), BF16),
                pltpu.VMEM((ys, m, 4, ffq // 2), BF16),
                pltpu.VMEM((ys, 4 * m, ff), F32),
                pltpu.VMEM((ys, reps - 1, 4 * m, ffq), F32),
                pltpu.VMEM((ys, 4 * m, ff), BF16),
                pltpu.VMEM((ys, m, 16, kc), BF16),
                pltpu.VMEM((ys, m, 16, kc), BF16),
                pltpu.VMEM((2, 2 * m * ys, width), BF16),
                pltpu.VMEM((16 * m, 16 * m), BF16),
                pltpu.VMEM((16 * m, 16 * m), BF16),
                pltpu.VMEM((4 * m, 4 * m), BF16),
                pltpu.VMEM((4 * m, 4 * m), BF16),
                dma,
            ]
            + [dma((ys,))] * 10,
            compiler_params=pltpu.CompilerParams(
                collective_id=0, has_side_effects=True, vmem_limit_bytes=48 * 1024 * 1024
            ),
        )(tokens, probe, cotangent, expert_ids, weight[0])

    in_specs = (
        P("expert", "replica"),
        P("expert", "replica"),
        P("expert", None),
        P("expert", None),
        P("expert", "replica", None),
    )
    out_specs = (P("expert", "replica"), P("expert", "replica"))
    return jax.shard_map(shards, mesh=mesh, in_specs=in_specs, out_specs=out_specs, check_vma=False)
```

time: 251 us -> 125 us (0.50)
  the two profiles are of different devices: /device:TPU:1 before, /device:TPU:16 now
where the time goes in v1:
time: 125 us; the launch traced here: 124 us
  Pallas kernels  117 us (94%)
  local copies, waits for them, and re-layouts  7.08 us (6%)
    pallas_call x1, Pallas kernels, shards(): pl.pallas_call(functools.partial(kernel, zs, ys, reps), out_shape=[jax.Sh...  117 us
    unnamed x11, local copies, waits for them, and re-layouts  7.08 us

profile of v1, /device:TPU:16, one launch (start us, length us, event | category | flops | bytes accessed | tf_op | source)
XLA Modules:
  0.0 124.3 jit_solution(1852584669979094415)
XLA Ops:
  0.6 0.8 copy.7.ids_ref
  1.4 0.0 copy-start
  1.4 1.9 %copy-done = bf16[1,1536,1024]{2,1,0:T(8,128)(2,1)S(1)} copy-done((bf16[1,1536,1024]{2,1,0:T(8,128)(2,1)S(1)}, bf16[1,1536,1024]{2,1,0:T(8,128)(2,1)}, u32[]{:S(2)}) %copy-start) | copy-done | bytes 3145752
  3.3 0.0 copy-start.1
  3.3 1.0 copy-done.1
  4.3 0.0 copy-start.2
  4.3 1.0 copy-done.2
  5.3 0.0 copy-start.3
  5.3 0.9 copy-done.3
  6.2 116.6 %shard_map.68 = (bf16[128,1536]{1,0:T(8,128)(2,1)S(1)}, bf16[128,1536]{1,0:T(8,128)(2,1)S(1)}) custom-call(bf16[128,1536]{1,0:T(8,128)(2,1)S(1)} %copy-done.1, bf16[128,1536]{1,0:T(8,128)(2,1)S(1)} %copy-done.2, bf16[128,1024]{1,0:T(8,128)(2,1)S(1)} %copy-done.3, s32[128,1]{1,0:T(8,128)S(1)} %copy.7.ids_ref, bf16[1536,1024]{1,0:T(8,128)(2,1)S(1)} %bitcast.1), custom_call_target="tpu_custom_call" | custom-call | tf_op jit(solution)/shard_map/pallas_call | solution.py:289
  122.8 0.7 copy.10
  123.5 0.7 copy.11
Async XLA Ops:
  1.4 1.9 %copy-start = (bf16[1,1536,1024]{2,1,0:T(8,128)(2,1)S(1)}, bf16[1,1536,1024]{2,1,0:T(8,128)(2,1)}, u32[]{:S(2)}) copy-start(bf16[1,1536,1024]{2,1,0:T(8,128)(2,1)} %param.9) | copy-start | bytes 9437188
  3.3 1.0 copy-start.1
  4.3 1.0 copy-start.2
  5.3 0.9 copy-start.3

commit v2 on v1

v2 whole, which is shorter than its diff:
```python
import functools

import jax
import jax.numpy as jnp
from jax import lax
from jax.experimental import pallas as pl
from jax.experimental.pallas import tpu as pltpu
from jax.sharding import PartitionSpec as P

CHUNKS = 4
AHEAD = 2
LAG_SUM = 1
LAG_BACK = 2
MESH = pl.DeviceIdType.MESH
F32 = jnp.float32
BF16 = jnp.bfloat16
LANES = 128


def mm(a, b):
    return jnp.dot(a, b, preferred_element_type=F32)


def iota(shape, dim):
    return lax.broadcasted_iota(jnp.int32, shape, dim)


def position(zs, ys):
    me = lax.axis_index("expert")
    return me, me // (2 * ys), lax.rem(me // 2, ys), lax.rem(me, 2)


def targets(zs, ys, ids_row, as_row):
    n = ids_row.shape[1]
    _, z, y, core = position(zs, ys)
    row, col = iota((n, n), 0), iota((n, n), 1)
    ids_col = jnp.sum(
        jnp.where(row == col, ids_row.astype(F32), 0.0), axis=1, keepdims=True
    ).astype(jnp.int32)
    same = ids_col == ids_row
    if as_row:
        slot = jnp.sum(jnp.where(same & (row < col), 1.0, 0.0), axis=0, keepdims=True)
        ids = ids_row
    else:
        slot = jnp.sum(jnp.where(same & (col < row), 1.0, 0.0), axis=1, keepdims=True)
        ids = ids_col
    to_core, to_y, to_z = ids % 2, (ids // 2) % ys, ids // (2 * ys)
    dz = (to_z - z + zs) % zs
    diagonal = (to_y - y - dz + (zs + 2) * ys) % ys
    block = (diagonal * zs + dz) * 2 + (to_core + core) % 2
    return 4 * block + slot.astype(jnp.int32)


def exchange(
    zs, ys, reps, chunks,
    x_hbm, p_hbm, cot_hbm, ids_hbm, w_hbm,
    rows_hbm,
    data, ids_ref, w, fsend, frecv, part, rsrecv, act, bsend, brecv, rows,
    in_sem, out_sem, f_ss, f_rs, r_ss, r_rs, a_ss, a_rs, b_ss, b_rs,
):
    experts = 2 * zs * ys
    m = experts // chunks
    n, width = x_hbm.shape
    tiles = width // LANES
    ffq = part.shape[2] // reps
    me, z, y, core = position(zs, ys)
    rep = lax.axis_index("replica")

    def partner(c, i, forward):
        block = c * m + i
        diagonal, dz, rc = block // (2 * zs), lax.rem(block // 2, zs), lax.rem(block, 2)
        if forward:
            zz, yy = lax.rem(z + dz, zs), lax.rem(y + dz + diagonal, ys)
        else:
            zz, yy = lax.rem(z + zs - dz, zs), lax.rem(y + (zs + 2) * ys - dz - diagonal, ys)
        return (zz * ys + yy) * 2 + lax.rem(core + rc, 2)

    def quarter(r):
        return pl.ds(pl.multiple_of(r * ffq, ffq), ffq)

    loads = [
        pltpu.make_async_copy(a, b, in_sem.at[i])
        for i, (a, b) in enumerate([
            (ids_hbm, ids_ref),
            (x_hbm, data.at[pl.ds(0, n), pl.ds(0, width)]),
            (p_hbm, data.at[pl.ds(n, n), pl.ds(0, width)]),
            (
                cot_hbm.at[:, pl.ds(pl.multiple_of(rep * ffq, LANES), LANES)],
                data.at[pl.ds(0, n), pl.ds(width, LANES)],
            ),
            (
                cot_hbm.at[:, pl.ds(pl.multiple_of(rep * ffq + LANES, LANES), LANES)],
                data.at[pl.ds(n, n), pl.ds(width, LANES)],
            ),
            (w_hbm, w),
        ])
    ]
    for load in loads:
        load.start()

    barrier = pltpu.get_barrier_semaphore()

    def greet(i, carry):
        pl.semaphore_signal(
            barrier, inc=1, device_id=(lax.rem(me + i, experts), rep), device_id_type=MESH
        )
        return carry

    for j in range(1, reps):
        pl.semaphore_signal(
            barrier, inc=1, device_id=(me, lax.rem(rep + j, reps)), device_id_type=MESH
        )
    lax.fori_loop(1, experts, greet, 0)

    loads[0].wait()
    tgt = targets(zs, ys, ids_ref[...], True)
    tgt = jnp.concatenate([tgt, tgt + 2], axis=1)
    for load in loads[1:5]:
        load.wait()

    def whole(ref, c, sem, own):
        if not own:
            pltpu.make_async_copy(ref.at[c], ref.at[c], sem.at[c]).wait()
            return

        @pl.when(c == 0)
        def _():
            some = ref.at[0, pl.ds(1, m - 1)]
            pltpu.make_async_copy(some, some, sem.at[0]).wait()

        @pl.when(c > 0)
        def _():
            pltpu.make_async_copy(ref.at[c], ref.at[c], sem.at[c]).wait()

    def others(ref, c, sem):
        some = ref.at[c, :, pl.ds(0, (reps - 1) * ffq)]
        pltpu.make_async_copy(some, some, sem.at[c]).wait()

    def spread(ref, c, value):
        for t in range(value.shape[1] // LANES):
            ref[c, :, t] = value[:, t * LANES:(t + 1) * LANES].reshape(m, 4, LANES)

    def gather(ref, c, count):
        return jnp.concatenate([ref[c, :, t].reshape(4 * m, LANES) for t in range(count)], axis=1)

    def exchange_blocks(src, dst, c, forward, ss, rs):
        @pl.when(c == 0)
        def _():
            dst[0, 0] = src[0, 0]

        def one(i, carry):
            pltpu.make_async_remote_copy(
                src_ref=src.at[c, i], dst_ref=dst.at[c, i],
                send_sem=ss.at[c], recv_sem=rs.at[c],
                device_id=(partner(c, i, forward), rep), device_id_type=MESH,
            ).start()
            return carry

        lax.fori_loop(jnp.where(c == 0, 1, 0), m, one, 0)

    def pack(c):
        route = jnp.where(iota((4 * m, 2 * n), 0) + c * (4 * m) == tgt, 1.0, 0.0).astype(BF16)
        spread(fsend, c, mm(route, data[...]).astype(BF16))

    def send(c):
        exchange_blocks(fsend, frecv, c, True, f_ss, f_rs)

    def project(c):
        whole(frecv, c, f_rs, True)
        part[c] = mm(gather(frecv, c, tiles), w[...])
        for j in range(1, reps):
            to = lax.rem(rep + j, reps)
            pltpu.make_async_remote_copy(
                src_ref=part.at[c, :, quarter(to)], dst_ref=rsrecv.at[c, j - 1],
                send_sem=r_ss.at[c], recv_sem=r_rs.at[c],
                device_id=(me, to), device_id_type=MESH,
            ).start()

    def activate(c):
        whole(rsrecv, c, r_rs, False)
        total = part[c, :, quarter(rep)]
        for j in range(reps - 1):
            total = total + rsrecv[c, j]
        early = iota((4 * m, 1), 0) % 4 < 2
        cot = frecv[c, :, tiles].reshape(4 * m, LANES).astype(F32)
        cot = jnp.concatenate(
            [
                jnp.where(early, cot, pltpu.roll(cot, 2, 0)),
                jnp.where(early, pltpu.roll(cot, 4 * m - 2, 0), cot),
            ],
            axis=1,
        )
        pre = jnp.where(early, total, pltpu.roll(total, 2, 0))
        sig = 1.0 / (1.0 + jnp.exp(-pre))
        first = sig * (1.0 + pre * (1.0 - sig))
        second = sig * (1.0 - sig) * (2.0 + pre * (1.0 - 2.0 * sig)) * total
        act[c, :, quarter(rep)] = (cot * jnp.where(early, first, second)).astype(BF16)
        for j in range(1, reps):
            to = lax.rem(rep + j, reps)
            pltpu.make_async_remote_copy(
                src_ref=act.at[c, :, quarter(rep)], dst_ref=act.at[c, :, quarter(rep)],
                send_sem=a_ss.at[c], recv_sem=a_rs.at[c],
                device_id=(me, to), device_id_type=MESH,
            ).start()

    def give_back(c):
        others(act, c, a_rs)
        back = lax.dot_general(
            act[c], w[...], (((1,), (1,)), ((), ())), preferred_element_type=F32
        )
        spread(bsend, c, back.astype(BF16))
        exchange_blocks(bsend, brecv, c, False, b_ss, b_rs)

    pack(0)
    pl.semaphore_wait(barrier, experts - 1 + reps - 1)
    send(0)

    def dispatch(c, carry):
        pack(c)
        send(c)
        return carry

    ahead = min(AHEAD, chunks)
    lax.fori_loop(1, ahead, dispatch, 0)
    loads[5].wait()

    def step(s, carry):
        @pl.when(s + ahead < chunks)
        def _():
            dispatch(s + ahead, 0)

        @pl.when(s < chunks)
        def _():
            project(s)

        @pl.when((s >= LAG_SUM) & (s < chunks + LAG_SUM))
        def _():
            activate(s - LAG_SUM)

        @pl.when(s >= LAG_BACK)
        def _():
            give_back(s - LAG_BACK)

        return carry

    lax.fori_loop(0, chunks + LAG_BACK, step, 0)

    def collect(c, carry):
        whole(brecv, c, b_rs, True)
        rows[c] = gather(brecv, c, tiles)
        pltpu.make_async_copy(rows.at[c], rows_hbm.at[c], out_sem).start()
        return carry

    lax.fori_loop(0, chunks, collect, 0)
    pltpu.make_async_copy(rows, rows_hbm, out_sem).wait()

    def drain(c, carry):
        whole(fsend, c, f_ss, True)
        whole(bsend, c, b_ss, True)
        others(part, c, r_ss)
        others(act, c, a_ss)
        return carry

    lax.fori_loop(0, chunks, drain, 0)


def combine(zs, ys, ids_ref, rows_ref, grad_ref, hv_ref):
    tgt = targets(zs, ys, ids_ref[...], False)
    n, count = tgt.shape[0], rows_ref.shape[0]
    tgt = jnp.concatenate([tgt, tgt + 2], axis=0)
    pick = jnp.where(iota((2 * n, count), 1) == tgt, 1.0, 0.0).astype(BF16)
    got = mm(pick, rows_ref[...]).astype(BF16)
    grad_ref[...] = got[:n]
    hv_ref[...] = got[n:]


def solution(mesh):
    experts, reps = mesh.shape["expert"], mesh.shape["replica"]
    zs = {128: 8, 8: 2}[experts]
    ys = experts // (2 * zs)
    chunks = min(CHUNKS, ys)
    m = experts // chunks

    def shards(tokens, probe, cotangent, expert_ids, weight):
        n, width = tokens.shape
        ff = weight.shape[2]
        ffq = ff // reps
        tiles = width // LANES
        anywhere = pl.BlockSpec(memory_space=pl.ANY)
        vmem = pl.BlockSpec(memory_space=pltpu.VMEM)
        dma = pltpu.SemaphoreType.DMA
        ids = expert_ids.reshape(1, n)
        rows = pl.pallas_call(
            functools.partial(exchange, zs, ys, reps, chunks),
            out_shape=jax.ShapeDtypeStruct((chunks, 4 * m, width), BF16),
            in_specs=[anywhere] * 5,
            out_specs=anywhere,
            scratch_shapes=[
                pltpu.VMEM((2 * n, width + LANES), BF16),
                pltpu.VMEM((1, n), jnp.int32),
                pltpu.VMEM((width, ff), BF16),
                pltpu.VMEM((chunks, m, tiles + 1, 4, LANES), BF16),
                pltpu.VMEM((chunks, m, tiles + 1, 4, LANES), BF16),
                pltpu.VMEM((chunks, 4 * m, ff), F32),
                pltpu.VMEM((chunks, reps - 1, 4 * m, ffq), F32),
                pltpu.VMEM((chunks, 4 * m, ff), BF16),
                pltpu.VMEM((chunks, m, tiles, 4, LANES), BF16),
                pltpu.VMEM((chunks, m, tiles, 4, LANES), BF16),
                pltpu.VMEM((chunks, 4 * m, width), BF16),
                dma((6,)),
                dma,
            ]
            + [dma((chunks,))] * 8,
            compiler_params=pltpu.CompilerParams(
                collective_id=0, has_side_effects=True, vmem_limit_bytes=60 * 1024 * 1024
            ),
        )(tokens, probe, cotangent, ids, weight[0])
        return pl.pallas_call(
            functools.partial(combine, zs, ys),
            out_shape=[jax.ShapeDtypeStruct((n, width), BF16)] * 2,
            in_specs=[vmem] * 2,
            out_specs=[vmem] * 2,
            compiler_params=pltpu.CompilerParams(vmem_limit_bytes=60 * 1024 * 1024),
        )(ids, rows.reshape(4 * experts, width))

    in_specs = (
        P("expert", "replica"),
        P("expert", "replica"),
        P("expert", None),
        P("expert", None),
        P("expert", "replica", None),
    )
    out_specs = (P("expert", "replica"), P("expert", "replica"))
    return jax.shard_map(shards, mesh=mesh, in_specs=in_specs, out_specs=out_specs, check_vma=False)
```

time: 125 us -> 104 us (0.83)
  the two profiles are of different devices: /device:TPU:16 before, /device:TPU:1 now
where the time goes in v2:
time: 104 us
  Pallas kernels  104 us (100%)
    pallas_call x1, Pallas kernels, shards(): pl.pallas_call(functools.partial(exchange, zs, ys, reps, chunks), out_sha...  100 us
    pallas_call x1, Pallas kernels, shards(): pl.pallas_call(functools.partial(combine, zs, ys), out_shape=[jax.ShapeDt...  3.18 us

profile of v2, /device:TPU:1, one launch (start us, length us, event | category | flops | bytes accessed | tf_op | source)
XLA Modules:
  0.0 104.2 jit_solution(8562610764624866691)
XLA Ops:
  0.6 100.4 %shard_map.68 = bf16[4,128,1536]{2,1,0:T(8,128)(2,1)} custom-call(bf16[128,1536]{1,0:T(8,128)(2,1)} %x_hbm.1, bf16[128,1536]{1,0:T(8,128)(2,1)} %p_hbm.1, bf16[128,1024]{1,0:T(8,128)(2,1)} %cot_hbm.1, s32[1,128]{1,0:T(1,128)} %bitcast.5, bf16[1536,1024]{1,0:T(8,128)(2,1)} %bitcast.4), custom_call_target="tpu_custom_call" | custom-call | tf_op jit(solution)/shard_map/pallas_call | solution.py:293
  101.1 3.2 %shard_map.69 = (bf16[128,1536]{1,0:T(8,128)(2,1)}, bf16[128,1536]{1,0:T(8,128)(2,1)}) custom-call(s32[1,128]{1,0:T(1,128)} %bitcast.6, bf16[512,1536]{1,0:T(8,128)(2,1)} %bitcast.3), custom_call_target="tpu_custom_call" | custom-call | tf_op jit(solution)/shard_map/pallas_call | solution.py:318

commit v3 on v2

v3 whole, which is shorter than its diff:
```python
import functools

import jax
import jax.numpy as jnp
from jax import lax
from jax.experimental import pallas as pl
from jax.experimental.pallas import tpu as pltpu
from jax.sharding import PartitionSpec as P

SIZES = (32, 32, 32, 32)
SCHEDULE = ""
AHEAD = 2
LAG_SUM = 1
LAG_BACK = 2
LAG_COLLECT = 4
MESH = pl.DeviceIdType.MESH
F32 = jnp.float32
BF16 = jnp.bfloat16
LANES = 128


def mm(a, b):
    return jnp.dot(a, b, preferred_element_type=F32)


def iota(shape, dim):
    return lax.broadcasted_iota(jnp.int32, shape, dim)


def position(zs, ys):
    me = lax.axis_index("expert")
    return me, me // (2 * ys), lax.rem(me // 2, ys), lax.rem(me, 2)


def targets(zs, ys, ids_row, as_row):
    n = ids_row.shape[1]
    _, z, y, core = position(zs, ys)
    row, col = iota((n, n), 0), iota((n, n), 1)
    ids_col = jnp.sum(
        jnp.where(row == col, ids_row.astype(F32), 0.0), axis=1, keepdims=True
    ).astype(jnp.int32)
    same = ids_col == ids_row
    if as_row:
        slot = jnp.sum(jnp.where(same & (row < col), 1.0, 0.0), axis=0, keepdims=True)
        ids = ids_row
    else:
        slot = jnp.sum(jnp.where(same & (col < row), 1.0, 0.0), axis=1, keepdims=True)
        ids = ids_col
    to_core, to_y, to_z = ids % 2, (ids // 2) % ys, ids // (2 * ys)
    dz = (to_z - z + zs) % zs
    diagonal = (to_y - y - dz + (zs + 2) * ys) % ys
    block = (diagonal * zs + dz) * 2 + (to_core + core) % 2
    return 4 * block + slot.astype(jnp.int32)


def plan(count):
    if count == len(SIZES) and SCHEDULE:
        return [(step[0], int(step[1:])) for step in SCHEDULE.split()]
    order = []
    for s in range(count + LAG_COLLECT):
        for name, lag in (
            ("D", -AHEAD), ("P", 0), ("A", LAG_SUM), ("B", LAG_BACK), ("C", LAG_COLLECT)
        ):
            first = range(min(AHEAD, count)) if s == 0 and name == "D" else ()
            order += [(name, c) for c in first]
            if 0 <= s - lag < count:
                order.append((name, s - lag))
    return order


def exchange(
    zs, ys, reps, sizes,
    x_hbm, p_hbm, cot_hbm, ids_hbm, w_hbm,
    grad_ref, hv_ref,
    data, ids_ref, w, fsend, frecv, part, rsrecv, act, bsend, brecv, total,
    in_sem, f_ss, f_rs, r_ss, r_rs, a_ss, a_rs, b_ss, b_rs,
):
    experts = 2 * zs * ys
    starts = [sum(sizes[:c]) for c in range(len(sizes))]
    n, width = x_hbm.shape
    tiles = width // LANES
    ffq = part.shape[1] // reps
    me, z, y, core = position(zs, ys)
    rep = lax.axis_index("replica")

    def partner(block, forward):
        diagonal, dz, rc = block // (2 * zs), lax.rem(block // 2, zs), lax.rem(block, 2)
        if forward:
            zz, yy = lax.rem(z + dz, zs), lax.rem(y + dz + diagonal, ys)
        else:
            zz, yy = lax.rem(z + zs - dz, zs), lax.rem(y + (zs + 2) * ys - dz - diagonal, ys)
        return (zz * ys + yy) * 2 + lax.rem(core + rc, 2)

    def quarter(r):
        return pl.ds(pl.multiple_of(r * ffq, ffq), ffq)

    def blocks_of(c):
        return pl.ds(starts[c], sizes[c])

    def sent_of(c):
        skip = 1 if c == 0 else 0
        return pl.ds(starts[c] + skip, sizes[c] - skip)

    def rows_of(c):
        return pl.ds(4 * starts[c], 4 * sizes[c])

    loads = [
        pltpu.make_async_copy(a, b, in_sem.at[i])
        for i, (a, b) in enumerate([
            (ids_hbm, ids_ref),
            (x_hbm, data.at[pl.ds(0, n), pl.ds(0, width)]),
            (p_hbm, data.at[pl.ds(n, n), pl.ds(0, width)]),
            (
                cot_hbm.at[:, pl.ds(pl.multiple_of(rep * ffq, LANES), LANES)],
                data.at[pl.ds(0, n), pl.ds(width, LANES)],
            ),
            (
                cot_hbm.at[:, pl.ds(pl.multiple_of(rep * ffq + LANES, LANES), LANES)],
                data.at[pl.ds(n, n), pl.ds(width, LANES)],
            ),
            (w_hbm, w),
        ])
    ]
    for load in loads[:5]:
        load.start()

    barrier = pltpu.get_barrier_semaphore()

    def greet(i, carry):
        pl.semaphore_signal(
            barrier, inc=1, device_id=(lax.rem(me + i, experts), rep), device_id_type=MESH
        )
        return carry

    for j in range(1, reps):
        pl.semaphore_signal(
            barrier, inc=1, device_id=(me, lax.rem(rep + j, reps)), device_id_type=MESH
        )
    lax.fori_loop(1, experts, greet, 0)

    loads[0].wait()
    tgt = targets(zs, ys, ids_ref[...], True)
    tgt = jnp.concatenate([tgt, tgt + 2], axis=1)
    tgt_col = targets(zs, ys, ids_ref[...], False)
    tgt_col = jnp.concatenate([tgt_col, tgt_col + 2], axis=0)
    for load in loads[1:5]:
        load.wait()
    loads[5].start()

    def wait(piece, sem):
        pltpu.make_async_copy(piece, piece, sem).wait()

    def others(ref, c):
        return ref.at[rows_of(c), pl.ds(0, (reps - 1) * ffq)]

    def spread(ref, c, value):
        for t in range(value.shape[1] // LANES):
            tile = value[:, t * LANES:(t + 1) * LANES]
            ref[blocks_of(c), t] = tile.reshape(sizes[c], 4, LANES)

    def gather(ref, c, count):
        return jnp.concatenate(
            [ref[blocks_of(c), t].reshape(4 * sizes[c], LANES) for t in range(count)], axis=1
        )

    def exchange_blocks(src, dst, c, forward, ss, rs):
        if c == 0:
            dst[0] = src[0]

        def one(block, carry):
            pltpu.make_async_remote_copy(
                src_ref=src.at[block], dst_ref=dst.at[block],
                send_sem=ss.at[c], recv_sem=rs.at[c],
                device_id=(partner(block, forward), rep), device_id_type=MESH,
            ).start()
            return carry

        lax.fori_loop(starts[c] + (1 if c == 0 else 0), starts[c] + sizes[c], one, 0)

    def to_replicas(src, dst, c, ss, rs):
        for j in range(1, reps):
            to = lax.rem(rep + j, reps)
            pltpu.make_async_remote_copy(
                src_ref=src(to), dst_ref=dst(j), send_sem=ss.at[c], recv_sem=rs.at[c],
                device_id=(me, to), device_id_type=MESH,
            ).start()

    def pack(c):
        at = iota((4 * sizes[c], 2 * n), 0) + 4 * starts[c]
        route = jnp.where(at == tgt, 1.0, 0.0).astype(BF16)
        spread(fsend, c, mm(route, data[...]).astype(BF16))

    def dispatch(c):
        pack(c)
        if c == 0:
            pl.semaphore_wait(barrier, experts - 1 + reps - 1)
        exchange_blocks(fsend, frecv, c, True, f_ss, f_rs)

    def project(c):
        if c == 0:
            loads[5].wait()
        wait(frecv.at[sent_of(c)], f_rs.at[c])
        part[rows_of(c)] = mm(gather(frecv, c, tiles), w[...])
        to_replicas(
            lambda to: part.at[rows_of(c), quarter(to)],
            lambda j: rsrecv.at[j - 1, rows_of(c)],
            c, r_ss, r_rs,
        )

    def activate(c):
        wait(rsrecv.at[:, rows_of(c)], r_rs.at[c])
        count = 4 * sizes[c]
        summed = part[rows_of(c), quarter(rep)]
        for j in range(reps - 1):
            summed = summed + rsrecv[j, rows_of(c)]
        early = iota((count, 1), 0) % 4 < 2
        cot = frecv[blocks_of(c), tiles].reshape(count, LANES).astype(F32)
        cot = jnp.concatenate(
            [
                jnp.where(early, cot, pltpu.roll(cot, 2, 0)),
                jnp.where(early, pltpu.roll(cot, count - 2, 0), cot),
            ],
            axis=1,
        )
        pre = jnp.where(early, summed, pltpu.roll(summed, 2, 0))
        sig = 1.0 / (1.0 + jnp.exp(-pre))
        first = sig * (1.0 + pre * (1.0 - sig))
        second = sig * (1.0 - sig) * (2.0 + pre * (1.0 - 2.0 * sig)) * summed
        act[rows_of(c), quarter(rep)] = (cot * jnp.where(early, first, second)).astype(BF16)
        mine = act.at[rows_of(c), quarter(rep)]
        to_replicas(lambda to: mine, lambda j: mine, c, a_ss, a_rs)

    def give_back(c):
        wait(others(act, c), a_rs.at[c])
        back = lax.dot_general(
            act[rows_of(c)], w[...], (((1,), (1,)), ((), ())), preferred_element_type=F32
        )
        spread(bsend, c, back.astype(BF16))
        exchange_blocks(bsend, brecv, c, False, b_ss, b_rs)

    def collect(c):
        wait(brecv.at[sent_of(c)], b_rs.at[c])
        at = iota((2 * n, 4 * sizes[c]), 1) + 4 * starts[c]
        pick = jnp.where(at == tgt_col, 1.0, 0.0).astype(BF16)
        got = mm(pick, gather(brecv, c, tiles))
        if c > 0:
            got = got + total[...]
        if c < len(sizes) - 1:
            total[...] = got
        else:
            grad_ref[...] = got[:n].astype(BF16)
            hv_ref[...] = got[n:].astype(BF16)

    steps = dict(D=dispatch, P=project, A=activate, B=give_back, C=collect)
    for name, c in plan(len(sizes)):
        steps[name](c)

    for c in range(len(sizes)):
        wait(fsend.at[sent_of(c)], f_ss.at[c])
        wait(bsend.at[sent_of(c)], b_ss.at[c])
        wait(others(part, c), r_ss.at[c])
        wait(others(act, c), a_ss.at[c])


def solution(mesh):
    experts, reps = mesh.shape["expert"], mesh.shape["replica"]
    zs = {128: 8, 8: 2}[experts]
    ys = experts // (2 * zs)
    sizes = SIZES if sum(SIZES) == experts else (2, 4, 2)
    count = len(sizes)

    def shards(tokens, probe, cotangent, expert_ids, weight):
        n, width = tokens.shape
        ff = weight.shape[2]
        ffq = ff // reps
        tiles = width // LANES
        outside = pl.BlockSpec(memory_space=pltpu.HBM)
        dma = pltpu.SemaphoreType.DMA
        return pl.pallas_call(
            functools.partial(exchange, zs, ys, reps, sizes),
            out_shape=[jax.ShapeDtypeStruct((n, width), BF16)] * 2,
            in_specs=[outside] * 5,
            out_specs=[pl.BlockSpec(memory_space=pltpu.VMEM)] * 2,
            scratch_shapes=[
                pltpu.VMEM((2 * n, width + LANES), BF16),
                pltpu.VMEM((1, n), jnp.int32),
                pltpu.VMEM((width, ff), BF16),
                pltpu.VMEM((experts, tiles + 1, 4, LANES), BF16),
                pltpu.VMEM((experts, tiles + 1, 4, LANES), BF16),
                pltpu.VMEM((4 * experts, ff), F32),
                pltpu.VMEM((reps - 1, 4 * experts, ffq), F32),
                pltpu.VMEM((4 * experts, ff), BF16),
                pltpu.VMEM((experts, tiles, 4, LANES), BF16),
                pltpu.VMEM((experts, tiles, 4, LANES), BF16),
                pltpu.VMEM((2 * n, width), F32),
                dma((6,)),
            ]
            + [dma((count,))] * 8,
            compiler_params=pltpu.CompilerParams(
                collective_id=0, has_side_effects=True, vmem_limit_bytes=44 * 1024 * 1024
            ),
        )(*[pltpu.with_memory_space_constraint(a, pltpu.HBM) for a in (tokens, probe, cotangent, expert_ids.reshape(1, n), weight[0])])

    in_specs = (
        P("expert", "replica"),
        P("expert", "replica"),
        P("expert", None),
        P("expert", None),
        P("expert", "replica", None),
    )
    out_specs = (P("expert", "replica"), P("expert", "replica"))
    return jax.shard_map(shards, mesh=mesh, in_specs=in_specs, out_specs=out_specs, check_vma=False)
```

time: 104 us -> 103 us (level)
  Pallas kernels: 104 us -> 100 us
  local copies, waits for them, and re-layouts: 0 us -> 1.49 us
    pallas_call x2 -> x1, Pallas kernels: 104 us -> 100 us  [shards(): pl.pallas_call(functools.partial(exchange, zs, ys, reps, sizes), out_shap...]
    unnamed x0 -> x2, local copies, waits for them, and re-layouts: none -> 1.49 us
where the time goes in v3:
time: 103 us; the launch traced here: 102 us
  Pallas kernels  100 us (97%)
  local copies, waits for them, and re-layouts  1.49 us (1%)
    pallas_call x1, Pallas kernels, shards(): pl.pallas_call(functools.partial(exchange, zs, ys, reps, sizes), out_shap...  100 us

profile of v3, /device:TPU:1, one launch (start us, length us, event | category | flops | bytes accessed | tf_op | source)
XLA Modules:
  0.0 102.4 jit_solution(10844282236276132419)
XLA Ops:
  0.6 100.3 %shard_map.68 = (bf16[128,1536]{1,0:T(8,128)(2,1)S(1)}, bf16[128,1536]{1,0:T(8,128)(2,1)S(1)}) custom-call(bf16[128,1536]{1,0:T(8,128)(2,1)} %x_hbm.1, bf16[128,1536]{1,0:T(8,128)(2,1)} %p_hbm.1, bf16[128,1024]{1,0:T(8,128)(2,1)} %cot_hbm.1, s32[1,128]{1,0:T(1,128)} %bitcast.3, bf16[1536,1024]{1,0:T(8,128)(2,1)} %bitcast.2), custom_call_target="tpu_custom_call" | custom-call | tf_op jit(solution)/shard_map/pallas_call | solution.py:279
  100.9 0.7 copy.9
  101.7 0.7 copy.10

commit v4 on v3

--- a/solution.py
+++ b/solution.py
@@ -7,12 +7,12 @@
 from jax.experimental.pallas import tpu as pltpu
 from jax.sharding import PartitionSpec as P
 
-SIZES = (32, 32, 32, 32)
+SIZES = (16, 16, 16, 16, 16, 16, 16, 16)
 SCHEDULE = ""
-AHEAD = 2
-LAG_SUM = 1
-LAG_BACK = 2
-LAG_COLLECT = 4
+AHEAD = 3
+LAG_SUM = 2
+LAG_BACK = 4
+LAG_COLLECT = 12
 MESH = pl.DeviceIdType.MESH
 F32 = jnp.float32
 BF16 = jnp.bfloat16
@@ -72,7 +72,7 @@
     zs, ys, reps, sizes,
     x_hbm, p_hbm, cot_hbm, ids_hbm, w_hbm,
     grad_ref, hv_ref,
-    data, ids_ref, w, fsend, frecv, part, rsrecv, act, bsend, brecv, total,
+    data, ids_ref, w, fsend, frecv, part, rsrecv, act, bsend, brecv, total, back_targets,
     in_sem, f_ss, f_rs, r_ss, r_rs, a_ss, a_rs, b_ss, b_rs,
 ):
     experts = 2 * zs * ys
@@ -141,8 +141,6 @@
     loads[0].wait()
     tgt = targets(zs, ys, ids_ref[...], True)
     tgt = jnp.concatenate([tgt, tgt + 2], axis=1)
-    tgt_col = targets(zs, ys, ids_ref[...], False)
-    tgt_col = jnp.concatenate([tgt_col, tgt_col + 2], axis=0)
     for load in loads[1:5]:
         load.wait()
     loads[5].start()
@@ -195,6 +193,9 @@
         if c == 0:
             pl.semaphore_wait(barrier, experts - 1 + reps - 1)
         exchange_blocks(fsend, frecv, c, True, f_ss, f_rs)
+        if c == len(sizes) - 1:
+            tgt_col = targets(zs, ys, ids_ref[...], False)
+            back_targets[...] = jnp.concatenate([tgt_col, tgt_col + 2], axis=0)
 
     def project(c):
         if c == 0:
@@ -239,6 +240,7 @@
         exchange_blocks(bsend, brecv, c, False, b_ss, b_rs)
 
     def collect(c):
+        tgt_col = back_targets[...]
         wait(brecv.at[sent_of(c)], b_rs.at[c])
         at = iota((2 * n, 4 * sizes[c]), 1) + 4 * starts[c]
         pick = jnp.where(at == tgt_col, 1.0, 0.0).astype(BF16)
@@ -293,6 +295,7 @@
                 pltpu.VMEM((experts, tiles, 4, LANES), BF16),
                 pltpu.VMEM((experts, tiles, 4, LANES), BF16),
                 pltpu.VMEM((2 * n, width), F32),
+                pltpu.VMEM((2 * n, 1), jnp.int32),
                 dma((6,)),
             ]
             + [dma((count,))] * 8,

time: 103 us -> 102 us (level)
  the two profiles are of different devices: /device:TPU:1 before, /device:TPU:49 now
where the time goes in v4:
time: 102 us
  Pallas kernels  99.8 us (98%)
  local copies, waits for them, and re-layouts  1.49 us (1%)
    pallas_call x1, Pallas kernels, shards(): pl.pallas_call(functools.partial(exchange, zs, ys, reps, sizes), out_shap...  99.8 us

profile of v4, /device:TPU:49, one launch (start us, length us, event | category | flops | bytes accessed | tf_op | source)
XLA Modules:
  0.0 102.0 jit_solution(12298333366839079676)
XLA Ops:
  0.6 99.8 %shard_map.68 = (bf16[128,1536]{1,0:T(8,128)(2,1)S(1)}, bf16[128,1536]{1,0:T(8,128)(2,1)S(1)}) custom-call(bf16[128,1536]{1,0:T(8,128)(2,1)} %x_hbm.1, bf16[128,1536]{1,0:T(8,128)(2,1)} %p_hbm.1, bf16[128,1024]{1,0:T(8,128)(2,1)} %cot_hbm.1, s32[1,128]{1,0:T(1,128)} %bitcast.3, bf16[1536,1024]{1,0:T(8,128)(2,1)} %bitcast.2), custom_call_target="tpu_custom_call" | custom-call | tf_op jit(solution)/shard_map/pallas_call | solution.py:281
  100.5 0.7 copy.9
  101.2 0.7 copy.10
